TPU v7x, 256 devices: a whole 4x4x8 slice. The times are simulated.
256 devices in a mesh: dp: 64 (over y, z, x_lo), mp: 4 (over x_hi, core).
Axes of the slice: x: 4 (x_hi: 2, x_lo: 2; x = x_hi * 2 + x_lo), y: 4, z: 8, core: 2. Of those that a mesh axis runs over, the one named last changes fastest.
Arguments:
- img_feat: bfloat16 [8192, 1536], P('dp', 'mp'), may hold values from -8 to 8
- txt_feat: bfloat16 [8192, 1152], P('dp', 'mp'), may hold values from -8 to 8
- img_proj: bfloat16 [1536, 1024], P('mp'), may hold values from -0.5 to 0.5
- txt_proj: bfloat16 [1152, 1024], P('mp'), may hold values from -0.5 to 0.5
- logit_scale: float32 [1], replicated, may hold values from 8 to 16
- logit_bias: float32 [1], replicated, may hold values from -8 to -3
Outputs:
- img_feat_grad: float32 [8192, 1536], P('dp', 'mp')
- txt_feat_grad: float32 [8192, 1152], P('dp', 'mp')
- img_proj_grad: float32 [1536, 1024], P('mp')
- txt_proj_grad: float32 [1152, 1024], P('mp')
All inputs are finite; a program needn't handle non-finite values.
Results may differ from a plain program's by a relative error of at most 0.0025.
Values may be sent and summed in bfloat16 or wider, within the bound.
A program may use at most 64 MiB of HBM per device.

v0:
```python
import math

import jax
import jax.numpy as jnp
from jax import lax
from jax.sharding import PartitionSpec as P


def normalize(full):
    norm = jnp.sqrt(jnp.sum(full * full, axis=1, keepdims=True) + 1e-06)
    return (full / norm, norm)


def back_norm(unit, norm, grad):
    inner = jnp.sum(unit * grad, axis=1, keepdims=True)
    return ((grad - unit * inner) / norm).astype(jnp.bfloat16)


def local(img_feat, txt_feat, img_proj, txt_proj, logit_scale, logit_bias):
    group_rows = img_feat.shape[0]
    emb_width = img_proj.shape[1]
    members = lax.axis_size("mp")
    cycle_size = lax.axis_size("dp")
    quarter = group_rows // members
    member = lax.axis_index("mp")
    position = lax.axis_index("dp")
    scale = logit_scale[0]
    offset = logit_bias[0]
    img_part = jnp.dot(img_feat, img_proj, preferred_element_type=jnp.float32)
    txt_part = jnp.dot(txt_feat, txt_proj, preferred_element_type=jnp.float32)
    img_full, txt_full = lax.psum((img_part, txt_part), "mp")
    img_unit, img_norm = normalize(img_full)
    txt_unit, txt_norm = normalize(txt_full)
    img_emb = img_unit.astype(jnp.bfloat16)
    own_txt = lax.dynamic_slice_in_dim(txt_unit, member * quarter, quarter, 0).astype(jnp.bfloat16)
    img_ids = position * group_rows + jnp.arange(group_rows, dtype=jnp.int32)

    def pair_terms(block, start):
        index = start + jnp.arange(block.shape[0], dtype=jnp.int32)
        ids = index // quarter * group_rows + member * quarter + index % quarter
        logits = (
            scale
            * lax.dot_general(
                img_emb, block, (((1,), (1,)), ((), ())), preferred_element_type=jnp.float32
            )
            + offset
        )
        sign = jnp.where(img_ids[:, None] == ids[None, :], jnp.float32(1.0), jnp.float32(-1.0))
        grad = (-sign * jax.nn.sigmoid(-sign * logits)).astype(jnp.bfloat16)
        img_term = scale * jnp.dot(grad, block, preferred_element_type=jnp.float32)
        txt_term = scale * lax.dot_general(
            grad, img_emb, (((0,), (0,)), ((), ())), preferred_element_type=jnp.float32
        )
        return (img_term, txt_term)

    empty_img = jnp.zeros((group_rows, emb_width), jnp.float32)
    texts = lax.all_gather(own_txt, "dp", axis=0, tiled=True)
    total = texts.shape[0]
    step_rows = math.gcd(512, total)
    blocks = total // step_rows

    def one_block(acc, item):
        index, block = item
        img_term, txt_term = pair_terms(block, index * step_rows)
        return (acc + img_term, txt_term)

    img_grad_part, txt_terms = lax.scan(
        one_block,
        empty_img,
        (jnp.arange(blocks, dtype=jnp.int32), texts.reshape(blocks, step_rows, emb_width)),
    )
    own_grad = lax.psum_scatter(
        txt_terms.reshape(total, emb_width), "dp", scatter_dimension=0, tiled=True
    )
    padded = lax.dynamic_update_slice_in_dim(
        jnp.zeros((group_rows, emb_width), jnp.float32), own_grad, member * quarter, 0
    )
    img_grad, txt_grad = lax.psum((img_grad_part, padded), "mp")
    img_du = back_norm(img_unit, img_norm, img_grad)
    txt_du = back_norm(txt_unit, txt_norm, txt_grad)
    img_feat_grad = jnp.dot(img_du, img_proj.T, preferred_element_type=jnp.float32)
    txt_feat_grad = jnp.dot(txt_du, txt_proj.T, preferred_element_type=jnp.float32)
    img_weight = lax.dot_general(
        img_feat, img_du, (((0,), (0,)), ((), ())), preferred_element_type=jnp.float32
    )
    txt_weight = lax.dot_general(
        txt_feat, txt_du, (((0,), (0,)), ((), ())), preferred_element_type=jnp.float32
    )
    img_sum, txt_sum = lax.psum((img_weight, txt_weight), "dp")
    root = jnp.sqrt(jnp.float32(group_rows * cycle_size))
    return (img_feat_grad, txt_feat_grad, img_sum / root, txt_sum / root)


def solution(mesh):
    placed = (P("dp", "mp"), P("dp", "mp"), P("mp", None), P("mp", None), P(), P())
    return jax.shard_map(
        local,
        mesh=mesh,
        in_specs=placed,
        out_specs=(P("dp", "mp"), P("dp", "mp"), P("mp", None), P("mp", None)),
        check_vma=False,
    )
```

profile of v0, /device:TPU:4, one launch (start us, length us, event | category | flops | bytes accessed | tf_op | source)
XLA Modules:
  0.0 1404.4 jit_solution(1434728246104519532)
XLA Ops:
  7.2 2.3 fusion.24
  9.5 2.0 fusion.25
  11.6 52.0 %all-reduce.11.cloned.1.call-done = (f32[128,1024]{1,0:T(8,128)}, f32[128,1024]{1,0:T(8,128)}) async-done(((f32[128,1024]{1,0:T(8,128)}, f32[128,1024]{1,0:T(8,128)}), (f32[128,1024]{1,0:T(8,128)}, f32[128,1024]{1,0:T(8,128)})) %all-reduce.11.cloned.1.call-update) | async-done | bytes 1048592 | tf_op jit(solution)/shard_map/psum | solution.py:31
  67.0 305.4 %all-gather.2.cloned.1.call-done = bf16[2048,1024]{1,0:T(8,128)(2,1)} async-done(((bf16[32,1024]{1,0:T(8,128)(2,1)}), bf16[2048,1024]{1,0:T(8,128)(2,1)}) %all-gather.2.cloned.1.call-update) | async-done | bytes 4194320 | tf_op jit(solution)/shard_map/all_gather | solution.py:57
  372.4 35.7 %while.15 = (s32[]{:T(128)}, f32[128,1024]{1,0:T(8,128)S(1)}, f32[4,512,1024]{2,1,0:T(8,128)}, f32[]{:T(128)}, s32[4]{0:T(128)S(1)}, /*index=5*/s32[]{:T(128)}, ...) while((s32[]{:T(128)}, f32[128,1024]{1,0:T(8,128)S(1)}, ...), condition=%wide.region_5.6_spmd.clone, body=%wide.region_4.5_spmd.clone.sunk | while | flops 404303488 | bytes 6169259 | solution.py:67
  373.7 3.0 fusion.60
  376.7 2.4 bitcast_dynamic-update-slice_fusion.2
  379.1 2.2 fusion.61
  382.6 3.0 fusion.60
  385.6 2.4 bitcast_dynamic-update-slice_fusion.2
  388.0 2.2 fusion.61
  391.5 3.0 fusion.60
  394.5 2.4 bitcast_dynamic-update-slice_fusion.2
  396.9 2.2 fusion.61
  400.4 3.0 fusion.60
  403.4 2.4 bitcast_dynamic-update-slice_fusion.2
  405.8 2.2 fusion.61
  408.9 330.0 %reduce-scatter.2.cloned.1.call-done = f32[32,1024]{1,0:T(8,128)} async-done(((f32[2048,1024]{1,0:T(8,128)}), f32[32,1024]{1,0:T(8,128)}) %reduce-scatter.2.cloned.1.call-update) | async-done | bytes 131088 | tf_op jit(solution)/shard_map/reduce_scatter | solution.py:72
  740.7 44.3 %all-reduce.9.cloned.1.call-done = (f32[128,1024]{1,0:T(8,128)}, f32[128,1024]{1,0:T(8,128)}) async-done(((f32[128,1024]{1,0:T(8,128)}, f32[128,1024]{1,0:T(8,128)}), (f32[128,1024]{1,0:T(8,128)}, f32[128,1024]{1,0:T(8,128)})) %all-reduce.9.cloned.1.call-update) | async-done | bytes 1048592 | tf_op jit(solution)/shard_map/psum | solution.py:78
  787.9 1.5 convolution_bitcast_fusion
  792.8 599.5 %all-reduce.7.cloned.1.call-done = (f32[384,1024]{0,1:T(8,128)}, f32[288,1024]{1,0:T(8,128)}) async-done(((f32[384,1024]{0,1:T(8,128)}, f32[288,1024]{1,0:T(8,128)}), (f32[384,1024]{0,1:T(8,128)}, f32[288,1024]{1,0:T(8,128)})) %all-reduce.7.cloned.1.call-update) | async-done | bytes 2752528 | tf_op jit(solution)/shard_map/psum | solution.py:89
  1392.3 1.5 broadcast_multiply_fusion
  1393.8 1.6 copy.10
  1395.4 2.5 broadcast_multiply_fusion.1
  (60 shorter events, 14.7 us)
Async XLA Ops:
  7.2 2.3 copy-start
  7.2 56.4 %all-reduce.11.cloned.1.call-start = ((), (), s32[]{:S(2)}) async-start(), calls=%async_computation.5 | async-start | bytes 2097152 | tf_op jit(solution)/shard_map/psum | solution.py:31
  11.5 360.9 %all-gather.2.cloned.1.call-start = ((), (), s32[]{:S(2)}) async-start(), calls=%async_computation.1 | async-start | bytes 4259840 | tf_op jit(solution)/shard_map/all_gather | solution.py:57
  63.6 3.1 copy-start.3
  66.7 672.2 %reduce-scatter.2.cloned.1.call-start = ((), (), s32[]{:S(2)}) async-start(), calls=%async_computation.2 | async-start | bytes 8519680 | tf_op jit(solution)/shard_map/reduce_scatter | solution.py:72
  408.1 0.8 copy-start.1
  408.9 377.5 %copy-start.2 = (f32[128,1024]{1,0:T(8,128)S(1)}, f32[128,1024]{1,0:T(8,128)}, u32[]{:S(2)}) copy-start(f32[128,1024]{1,0:T(8,128)} %get-tuple-element.201) | copy-start | bytes 1572868
  408.9 376.1 %all-reduce.9.cloned.1.call-start = ((), (), s32[]{:S(2)}) async-start(), calls=%async_computation.4 | async-start | bytes 2097152 | tf_op jit(solution)/shard_map/psum | solution.py:78
  739.8 0.8 copy-start.7
  740.7 651.6 %all-reduce.7.cloned.1.call-start = ((), (), s32[]{:S(2)}) async-start(), calls=%async_computation.3 | async-start | bytes 5505024 | tf_op jit(solution)/shard_map/psum | solution.py:89
  785.0 2.6 copy-start.5
  785.0 2.6 copy-start.6
  786.3 1.6 copy-start.8
  787.6 1.8 copy-start.9
  789.4 1.3 copy-start.4
Sparse Core Ops, SparseCore 0:
  11.6 51.9 all-reduce.10
  66.8 305.5 all-gather.1
  408.2 330.5 reduce-scatter.1
  742.2 42.7 all-reduce.8
  790.9 601.3 all-reduce.6
where the time goes:
time: 1410 us; the launch traced here: 1400 us
  waiting for transfers between devices  1330 us (94%)
  matrix products  39.6 us (3%)
    psum x1, waiting for transfers between devices, local(): img_sum, txt_sum = lax.psum((img_weight, txt_weight), 'dp')  599 us
    reduce_scatter x1, waiting for transfers between devices, local(): lax.psum_scatter(txt_terms.reshape(total, emb_width), 'dp', scatter_dimen...  330 us
    all_gather x1, waiting for transfers between devices, local(): texts = lax.all_gather(own_txt, 'dp', axis=0, tiled=True)  305 us
    psum x1, waiting for transfers between devices, local(): img_full, txt_full = lax.psum((img_part, txt_part), 'mp')  52 us
    psum x1, waiting for transfers between devices, local(): img_grad, txt_grad = lax.psum((img_grad_part, padded), 'mp')  44.3 us
  transfers between devices with their start and end apart: 5, of which 5 were waited for; matrix products, arithmetic and copies ran while one was open for 0% of the time, Pallas kernels for 0%

commit v1 on v0

v1 whole, which is shorter than its diff:
```python
import functools

import jax
import jax.numpy as jnp
from jax import lax
from jax.experimental import pallas as pl
from jax.experimental.pallas import tpu as pltpu
from jax.sharding import PartitionSpec as P

MESH = pl.DeviceIdType.MESH
F32 = jnp.float32
BF16 = jnp.bfloat16

NY, NZ, NXL, NXH, NC = 4, 8, 2, 2, 2
SIZE = {"y": NY, "z": NZ, "xl": NXL, "xh": NXH, "c": NC}
TEXT = ("xh", "xl", "y")
HEAD = ("z", "xl")
NTEXT = NXH * NXL * NY
NHEAD = NZ * NXL
MEMBERS = NXH * NC

NT = (((1,), (1,)), ((), ()))
TN = (((0,), (0,)), ((), ()))


def position():
    dp, mp = lax.axis_index("dp"), lax.axis_index("mp")
    return {
        "y": dp // (NZ * NXL),
        "z": (dp // NXL) % NZ,
        "xl": dp % NXL,
        "xh": mp // NC,
        "c": mp % NC,
    }


def shifted(me, axes, step, back=False):
    out = dict(me)
    for axis in reversed(axes):
        n = SIZE[axis]
        digit = lax.rem(step, n)
        step = step // n
        out[axis] = lax.rem(me[axis] + (n - digit if back else digit), n)
    return out


def address(at):
    return {
        "dp": (at["y"] * NZ + at["z"]) * NXL + at["xl"],
        "mp": at["xh"] * NC + at["c"],
    }


def send(src, dst, send_sem, recv_sem, to):
    return pltpu.make_async_remote_copy(
        src_ref=src,
        dst_ref=dst,
        send_sem=send_sem,
        recv_sem=recv_sem,
        device_id=address(to),
        device_id_type=MESH,
    )


def each(low, high, body):
    def step(k, _):
        body(k)
        return 0

    lax.fori_loop(low, high, step, 0)


def dot(a, b, dims=(((1,), (0,)), ((), ()))):
    return lax.dot_general(a, b, dims, preferred_element_type=F32)


def kernel(
    scale_ref, offset_ref, img_feat, txt_feat, img_proj, txt_proj,
    img_feat_out, txt_feat_out, img_proj_out, txt_proj_out,
    part, level1, relay, level2, unit, norm,
    img_emb, txt_emb, pair, sib_send, sib_recv,
    img_send, img_recv, txt_send, txt_recv, own,
    du, du_cols, img_all, txt_all, head_send, head_recv, heads,
    part_ss, part_rs, relay_ss, relay_rs, img_ss, img_rs, fwd_ss, fwd_rs, txt_ss, txt_rs,
    sib_ss, sib_rs, imgb_ss, imgb_rs, txtb_ss, txtb_rs, du_ss, du_rs, duf_ss, duf_rs,
    col_ss, col_rs, feat_ss, feat_rs, head_ss, head_rs, out_ss, out_rs, fin_ss, fin_rs,
):
    me = position()
    rows = unit.shape[1]
    width = unit.shape[2]
    cols = width // NY
    member = me["xh"] * NC + me["c"]
    scale = scale_ref[0]
    offset = offset_ref[0]
    sib = shifted(me, ("c",), 1)
    opp = shifted(me, ("xh",), 1)

    barrier = pltpu.get_barrier_semaphore()

    def greet(to):
        pl.semaphore_signal(barrier, inc=1, device_id=address(to), device_id_type=MESH)

    greet(sib)
    each(1, NZ, lambda k: greet(shifted(me, ("z",), k)))
    each(1, NTEXT, lambda k: greet(shifted(me, TEXT, k)))

    def greet_head(k):
        at = shifted(me, ("z",), k)
        greet(shifted(at, ("xl",), 1))

    each(0, NZ, greet_head)

    def partial(a, feat, proj):
        whole = dot(feat[...], proj[...])
        for q in range(MEMBERS):
            part[a, q % NC, q // NC] = whole[q * rows : (q + 1) * rows]

    partial(0, img_feat, img_proj)
    pl.semaphore_wait(barrier, 1 + (NZ - 1) + (NTEXT - 1) + NZ)

    def part_copy(a):
        return send(part.at[a, 1 - me["c"]], level1.at[a], part_ss.at[a], part_rs.at[a], sib)

    def relay_copy(a):
        return send(relay.at[a], level2.at[a], relay_ss.at[a], relay_rs.at[a], opp)

    part_copy(0).start()
    partial(1, txt_feat, txt_proj)
    part_copy(1).start()
    for a in range(2):
        part_copy(a).wait_recv()
        relay[a] = part[a, me["c"], 1 - me["xh"]] + level1[a, 1 - me["xh"]]
        relay_copy(a).start()

    img_all[0] = img_feat[...]
    txt_all[0] = txt_feat[...]

    def feat_copy(a, k):
        ref = (img_all, txt_all)[a]
        src = (img_feat, txt_feat)[a]
        return send(src, ref.at[k], feat_ss.at[a, k], feat_rs.at[a, k], shifted(me, ("y",), k))

    for a in range(2):
        each(1, NY, lambda k: feat_copy(a, k).start())

    def at_slot(k):
        return pl.ds(pl.multiple_of(k * rows, rows), rows)

    def embed(a, ref):
        relay_copy(a).wait_recv()
        full = part[a, me["c"], me["xh"]] + level1[a, me["xh"]] + level2[a]
        length = jnp.sqrt(jnp.sum(full * full, axis=1, keepdims=True) + 1e-06)
        value = full / length
        unit[a] = value
        norm[a] = jnp.broadcast_to(length, norm.shape[1:])
        ref[0:rows] = value.astype(BF16)

    def img_copy(k):
        return send(
            img_emb.at[0:rows], img_emb.at[at_slot(k)], img_ss.at[k], img_rs.at[k],
            shifted(me, ("z",), k),
        )

    def fwd_copy(k):
        return send(
            img_emb.at[at_slot(k)], img_emb.at[at_slot(NZ + k)], fwd_ss.at[k], fwd_rs.at[k], sib
        )

    def txt_copy(k):
        return send(
            txt_emb.at[0:rows], txt_emb.at[at_slot(k)], txt_ss.at[k], txt_rs.at[k],
            shifted(me, TEXT, k),
        )

    embed(0, img_emb)
    each(1, NZ, lambda k: img_copy(k).start())
    fwd_copy(0).start()
    embed(1, txt_emb)
    each(1, NTEXT, lambda k: txt_copy(k).start())

    def forward(k):
        img_copy(k).wait_recv()
        fwd_copy(k).start()

    each(1, NZ, forward)
    each(1, NTEXT, lambda k: txt_copy(k).wait_recv())
    each(0, NZ, lambda k: fwd_copy(k).wait_recv())

    half = NZ * rows
    txt_block = txt_emb[...]
    z = scale * dot(img_emb[...], txt_block, NT) + offset
    pair[...] = jax.nn.sigmoid(z).astype(BF16)
    corner = z[0:rows, 0:128]
    same = lax.broadcasted_iota(jnp.int32, corner.shape, 0) == lax.broadcasted_iota(
        jnp.int32, corner.shape, 1
    )
    pair[0:rows, 0:128] = jnp.where(
        same, -jax.nn.sigmoid(-corner), jax.nn.sigmoid(corner)
    ).astype(BF16)

    sib_copy = send(sib_send, sib_recv, sib_ss, sib_rs, sib)
    sib_send[...] = dot(pair[half : 2 * half], txt_block)
    sib_copy.start()

    def txtb_copy(k):
        return send(
            txt_send.at[at_slot(k)], txt_recv.at[k], txtb_ss.at[k], txtb_rs.at[k],
            shifted(me, TEXT, k, back=True),
        )

    def imgb_copy(k):
        return send(
            img_send.at[at_slot(k)], img_recv.at[k], imgb_ss.at[k], imgb_rs.at[k],
            shifted(me, ("z",), k, back=True),
        )

    txt_part = dot(pair[...], img_emb[...], TN)
    own[1] = txt_part[0:rows]
    txt_send[...] = txt_part.astype(BF16)
    each(1, NTEXT, lambda k: txtb_copy(k).start())
    img_part = dot(pair[0:half], txt_block)
    sib_copy.wait_recv()
    img_sum = img_part + sib_recv[...]
    own[0] = img_sum[0:rows]
    img_send[...] = img_sum.astype(BF16)
    each(1, NZ, lambda k: imgb_copy(k).start())

    def collect(a, copy, ref, count):
        def add(k, _):
            copy(k).wait_recv()
            own[a] += ref[k].astype(F32)
            return 0

        lax.fori_loop(1, count, add, 0)
        grad = scale * own[a]
        value = unit[a]
        inner = jnp.sum(value * grad, axis=1, keepdims=True)
        out = ((grad - value * inner) / norm[a, :, 0:1]).astype(BF16)
        for j in range(NY):
            du[member, j, a] = out[:, j * cols : (j + 1) * cols]

    collect(0, imgb_copy, img_recv, NZ)
    collect(1, txtb_copy, txt_recv, NTEXT)

    def block(q):
        return du.at[q]

    opp_copy = send(block(member), block(member), du_ss.at[0], du_rs.at[0], opp)
    near_copy = send(block(member), block(member), du_ss.at[1], du_rs.at[1], sib)
    far = opp["xh"] * NC + opp["c"]
    far_copy = send(block(far), block(far), duf_ss, duf_rs, sib)
    opp_copy.start()
    near_copy.start()
    opp_copy.wait_recv()
    far_copy.start()
    near_copy.wait_recv()
    far_copy.wait_recv()

    def col_copy(k):
        to = shifted(me, ("y",), k)
        return send(du.at[:, to["y"]], du_cols.at[k], col_ss.at[k], col_rs.at[k], to)

    each(1, NY, lambda k: col_copy(k).start())
    du_cols[0] = du[:, me["y"]]

    group = MEMBERS * rows
    for a, proj, out in ((0, img_proj, img_feat_out), (1, txt_proj, txt_feat_out)):
        total = None
        for j in range(NY):
            term = dot(du[:, j, a].reshape(group, cols), proj[:, j * cols : (j + 1) * cols], NT)
            total = term if total is None else total + term
        out[...] = total

    for a in range(2):
        each(1, NY, lambda k: feat_copy(a, k).wait_recv())
    each(1, NY, lambda k: col_copy(k).wait_recv())

    lanes = cols // NXL
    img_rows = img_proj_out.shape[0] // NZ
    piece = head_send.shape[2]
    txt_rows = piece - img_rows
    txt_holders = txt_proj_out.shape[0] // txt_rows

    def weight(a, ref):
        total = None
        for k in range(NY):
            term = dot(ref[k], du_cols[k, :, a].reshape(group, cols), TN)
            total = term if total is None else total + term
        return total

    root = jnp.sqrt(F32(group * NY * NZ * NXL))
    img_weight = weight(0, img_all).astype(BF16)
    txt_weight = weight(1, txt_all).astype(BF16)
    for s in range(NXL):
        for h in range(NZ):
            head_send[s, h, 0:img_rows] = img_weight[
                h * img_rows : (h + 1) * img_rows, s * lanes : (s + 1) * lanes
            ]
            if h < txt_holders:
                head_send[s, h, img_rows:piece] = txt_weight[
                    h * txt_rows : (h + 1) * txt_rows, s * lanes : (s + 1) * lanes
                ]
            else:
                head_send[s, h, img_rows:piece] = jnp.zeros((txt_rows, lanes), BF16)

    def head_copy(k):
        to = shifted(me, HEAD, k)
        return send(
            head_send.at[to["xl"], to["z"]], head_recv.at[k], head_ss.at[k], head_rs.at[k], to
        )

    each(1, NHEAD, lambda k: head_copy(k).start())

    def head_add(k, total):
        head_copy(k).wait_recv()
        return total + head_recv[k].astype(F32)

    total = lax.fori_loop(1, NHEAD, head_add, head_send[me["xl"], me["z"]].astype(F32))
    heads[me["y"], me["xl"], me["z"]] = (total / root).astype(BF16)

    def out_copy(k):
        at = heads.at[me["y"], me["xl"], me["z"]]
        return send(at, at, out_ss.at[k], out_rs.at[k], shifted(me, HEAD, k))

    def out_arrival(k):
        frm = shifted(me, HEAD, k, back=True)
        at = heads.at[me["y"], frm["xl"], frm["z"]]
        return send(at, at, out_ss.at[k], out_rs.at[k], shifted(me, HEAD, k))

    each(1, NHEAD, lambda k: out_copy(k).start())
    each(1, NHEAD, lambda k: out_arrival(k).wait_recv())

    def fin_copy(k):
        at = heads.at[me["y"]]
        return send(at, at, fin_ss.at[k], fin_rs.at[k], shifted(me, ("y",), k))

    def fin_arrival(k):
        at = heads.at[shifted(me, ("y",), k, back=True)["y"]]
        return send(at, at, fin_ss.at[k], fin_rs.at[k], shifted(me, ("y",), k))

    each(1, NY, lambda k: fin_copy(k).start())
    each(1, NY, lambda k: fin_arrival(k).wait_recv())
    for j in range(NY):
        for s in range(NXL):
            lane = slice((j * NXL + s) * lanes, (j * NXL + s + 1) * lanes)
            for h in range(NZ):
                img_proj_out[h * img_rows : (h + 1) * img_rows, lane] = heads[j, s, h, 0:img_rows]
                if h < txt_holders:
                    txt_proj_out[h * txt_rows : (h + 1) * txt_rows, lane] = heads[
                        j, s, h, img_rows:piece
                    ]

    for a in range(2):
        part_copy(a).wait_send()
        relay_copy(a).wait_send()
        each(1, NY, lambda k: feat_copy(a, k).wait_send())
    each(1, NZ, lambda k: img_copy(k).wait_send())
    each(0, NZ, lambda k: fwd_copy(k).wait_send())
    each(1, NTEXT, lambda k: txt_copy(k).wait_send())
    sib_copy.wait_send()
    each(1, NZ, lambda k: imgb_copy(k).wait_send())
    each(1, NTEXT, lambda k: txtb_copy(k).wait_send())
    opp_copy.wait_send()
    near_copy.wait_send()
    far_copy.wait_send()
    each(1, NY, lambda k: col_copy(k).wait_send())
    each(1, NHEAD, lambda k: head_copy(k).wait_send())
    each(1, NHEAD, lambda k: out_copy(k).wait_send())
    each(1, NY, lambda k: fin_copy(k).wait_send())


def local(img_feat, txt_feat, img_proj, txt_proj, logit_scale, logit_bias):
    group, img_width = img_feat.shape
    txt_width = txt_feat.shape[1]
    width = img_proj.shape[1]
    rows = group // MEMBERS
    cols = width // NY
    lanes = cols // NXL
    img_rows = img_width // NZ
    txt_rows = -(-txt_width // NZ // 16) * 16
    piece = img_rows + txt_rows
    dma = pltpu.SemaphoreType.DMA
    vmem = pltpu.VMEM

    def pair(*shape):
        return [dma(shape), dma(shape)]

    scratch = [
        vmem((2, NC, NXH, rows, width), F32),
        vmem((2, NXH, rows, width), F32),
        vmem((2, rows, width), F32),
        vmem((2, rows, width), F32),
        vmem((2, rows, width), F32),
        vmem((2, rows, 128), F32),
        vmem((NC * NZ * rows, width), BF16),
        vmem((NTEXT * rows, width), BF16),
        vmem((NC * NZ * rows, NTEXT * rows), BF16),
        vmem((NZ * rows, width), F32),
        vmem((NZ * rows, width), F32),
        vmem((NZ * rows, width), BF16),
        vmem((NZ, rows, width), BF16),
        vmem((NTEXT * rows, width), BF16),
        vmem((NTEXT, rows, width), BF16),
        vmem((2, rows, width), F32),
        vmem((MEMBERS, NY, 2, rows, cols), BF16),
        vmem((NY, MEMBERS, 2, rows, cols), BF16),
        vmem((NY, group, img_width), BF16),
        vmem((NY, group, txt_width), BF16),
        vmem((NXL, NZ, piece, lanes), BF16),
        vmem((NHEAD, piece, lanes), BF16),
        vmem((NY, NXL, NZ, piece, lanes), BF16),
        *pair(2), *pair(2), *pair(NZ), *pair(NZ), *pair(NTEXT),
        dma(()), dma(()), *pair(NZ), *pair(NTEXT), *pair(2), dma(()), dma(()),
        *pair(NY), *pair(2, NY), *pair(NHEAD), *pair(NHEAD), *pair(NY),
    ]
    in_vmem = pl.BlockSpec(memory_space=pltpu.VMEM)
    in_smem = pl.BlockSpec(memory_space=pltpu.SMEM)
    img_grad, txt_grad, img_sum, txt_sum = pl.pallas_call(
        kernel,
        out_shape=(
            jax.ShapeDtypeStruct((group, img_width), F32),
            jax.ShapeDtypeStruct((group, txt_width), F32),
            jax.ShapeDtypeStruct((img_width, width), BF16),
            jax.ShapeDtypeStruct((txt_width, width), BF16),
        ),
        in_specs=[in_smem, in_smem] + [in_vmem] * 4,
        out_specs=(in_vmem,) * 4,
        scratch_shapes=scratch,
        compiler_params=pltpu.CompilerParams(
            collective_id=0, has_side_effects=True, vmem_limit_bytes=48 * 2**20
        ),
        name="pair_loss",
    )(logit_scale, logit_bias, img_feat, txt_feat, img_proj, txt_proj)
    return img_grad, txt_grad, img_sum.astype(F32), txt_sum.astype(F32)


def solution(mesh):
    placed = (P("dp", "mp"), P("dp", "mp"), P("mp", None), P("mp", None), P(), P())
    return jax.shard_map(
        local,
        mesh=mesh,
        in_specs=placed,
        out_specs=(P("dp", "mp"), P("dp", "mp"), P("mp", None), P("mp", None)),
        check_vma=False,
    )
```

time: 1410 us -> 124 us (0.09)
  waiting for transfers between devices: 1330 us -> 0 us
  Pallas kernels: 0 us -> 114 us
  matrix products: 39.6 us -> 0 us
    psum x3 -> x0, waiting for transfers between devices: 696 us -> none  [the longest x1 599 us: local(): img_sum, txt_sum = lax.psum((img_weight, txt_weight), 'dp')]
    reduce_scatter x1 -> x0, waiting for transfers between devices: 330 us -> none  [local(): lax.psum_scatter(txt_terms.reshape(total, emb_width), 'dp', scatter_dimen...]
    all_gather x1 -> x0, waiting for transfers between devices: 305 us -> none  [local(): texts = lax.all_gather(own_txt, 'dp', axis=0, tiled=True)]
    pallas_call x0 -> x1, Pallas kernels: none -> 114 us  [local(): pl.pallas_call(kernel, out_shape=(jax.ShapeDtypeStruct((group, img_width)...]
    dot_general x18 -> x0, matrix products: 39.6 us -> none  [the longest x4 11.9 us: pair_terms(): lax.dot_general(img_emb, block, (((1,), (1,)), ((), ())), preferred_eleme...]
  transfers between devices with their start and end apart: 5 -> 0, of which waited for: 5 -> 0; matrix products, arithmetic and copies ran while one was open for 0% -> 0% of each run, Pallas kernels for 0% -> 0%
where the time goes in v1:
time: 124 us
  Pallas kernels  114 us (92%)
  local copies, waits for them, and re-layouts  5.53 us (4%)
  other arithmetic  2.46 us (2%)
  between operations  1.95 us (2%)
    pallas_call x1, Pallas kernels, local(): pl.pallas_call(kernel, out_shape=(jax.ShapeDtypeStruct((group, img_width)...  114 us
    unnamed x9, local copies, waits for them, and re-layouts  5.53 us

profile of v1, /device:TPU:4, one launch (start us, length us, event | category | flops | bytes accessed | tf_op | source)
XLA Modules:
  0.0 123.8 jit_solution(15138859687976648141)
XLA Ops:
  1.9 1.0 copy.10.txt_feat
  2.9 0.0 copy-start
  2.9 1.1 copy-done
  4.1 0.0 copy-start.1
  4.1 1.1 copy-done.1
  5.1 0.0 copy-start.2
  5.1 0.9 copy-done.2
  6.0 113.9 %pair_loss.1 = (f32[128,384]{1,0:T(8,128)S(1)}, f32[128,288]{1,0:T(8,128)S(1)}, bf16[384,1024]{1,0:T(8,128)(2,1)S(1)}, bf16[288,1024]{1,0:T(8,128)(2,1)S(1)}) custom-call(f32[1]{0:T(128)S(6)} %copy.13.scale_ref, f32[1]{0:T(128)S(6)} %copy.14.offset_ref, bf16[128,384]{1,0:T(8,128)(2,1)S(1)} %copy-done.2, bf16[128,288]{1,0:T(8,128)(2,1)S(1)} %copy.10.txt_feat, ...), custom_call_target="tpu_custom_call" | custom-call | tf_op jit(solution)/shard_map/pair_loss/pallas_call | solution.py:418
  119.9 0.8 copy.11
  120.7 1.3 %convert_element_type.6 = f32[384,1024]{1,0:T(8,128)} convert(bf16[384,1024]{1,0:T(8,128)(2,1)S(1)} %get-tuple-element.10) | non-fusion elementwise | flops 393216 | bytes 2359296 | tf_op jit(solution)/shard_map/convert_element_type | solution.py:434
  122.0 1.1 convert_element_type.7
  123.1 0.7 copy.15
Async XLA Ops:
  2.9 1.1 copy-start
  4.1 1.1 copy-start.1
  5.1 0.9 copy-start.2
